TPU v7x, 32 devices: a whole 2x2x4 slice. The times are simulated.
32 devices in a mesh: dp: 8 (over z, x), tensor: 4 (over y, core).
Axes of the slice: x: 2, y: 2, z: 4, core: 2. Of those that a mesh axis runs over, the one named last changes fastest.
Arguments:
- states: bfloat16 [8, 1024, 768], P('dp', 'tensor'), may hold values from -6 to 6
- encoder: bfloat16 [8, 512, 768], P('dp', 'tensor'), may hold values from -6 to 6
- upstream: bfloat16 [8, 1024, 768], P('dp', 'tensor'), may hold values from -6 to 6
- decoder_docs: int32 [8, 1024], P('dp'), may hold values from 0 to 3, as said below
- encoder_docs: int32 [8, 512], P('dp'), may hold values from 0 to 3, as said below
- norm_self: float32 [768], replicated, may hold values from 0.25 to 1.75
- norm_cross: float32 [768], replicated, may hold values from 0.25 to 1.75
- norm_feed: float32 [768], replicated, may hold values from 0.25 to 1.75
- position_table: float32 [32, 12], replicated, may hold values from -4 to 4
- self_query: bfloat16 [768, 768], P('dp', 'tensor'), may hold values from -0.0546875 to 0.0546875
- self_key: bfloat16 [768, 768], P('dp', 'tensor'), may hold values from -0.21875 to 0.21875
- self_value: bfloat16 [768, 768], P('dp', 'tensor'), may hold values from -0.21875 to 0.21875
- self_output: bfloat16 [768, 768], P('tensor', 'dp'), may hold values from -0.625 to 0.625
- cross_query: bfloat16 [768, 768], P('dp', 'tensor'), may hold values from -0.0546875 to 0.0546875
- cross_key: bfloat16 [768, 768], P('dp', 'tensor'), may hold values from -0.21875 to 0.21875
- cross_value: bfloat16 [768, 768], P('dp', 'tensor'), may hold values from -0.21875 to 0.21875
- cross_output: bfloat16 [768, 768], P('tensor', 'dp'), may hold values from -0.625 to 0.625
- feed_gate: bfloat16 [768, 2048], P('dp', 'tensor'), may hold values from -0.21875 to 0.21875
- feed_up: bfloat16 [768, 2048], P('dp', 'tensor'), may hold values from -0.21875 to 0.21875
- feed_down: bfloat16 [2048, 768], P('tensor', 'dp'), may hold values from -0.125 to 0.125
Outputs:
- layer_output: bfloat16 [8, 1024, 768], P('dp', 'tensor')
- states_gradient: float32 [8, 1024, 768], P('dp', 'tensor')
- encoder_gradient: float32 [8, 512, 768], P('dp', 'tensor')
- norm_self_gradient: float32 [768], replicated
- norm_cross_gradient: float32 [768], replicated
- norm_feed_gradient: float32 [768], replicated
- table_gradient: float32 [32, 12], replicated
- self_query_gradient: float32 [768, 768], P('dp', 'tensor')
- self_key_gradient: float32 [768, 768], P('dp', 'tensor')
- self_value_gradient: float32 [768, 768], P('dp', 'tensor')
- self_output_gradient: float32 [768, 768], P('tensor', 'dp')
- cross_query_gradient: float32 [768, 768], P('dp', 'tensor')
- cross_key_gradient: float32 [768, 768], P('dp', 'tensor')
- cross_value_gradient: float32 [768, 768], P('dp', 'tensor')
- cross_output_gradient: float32 [768, 768], P('tensor', 'dp')
- feed_gate_gradient: float32 [768, 2048], P('dp', 'tensor')
- feed_up_gradient: float32 [768, 2048], P('dp', 'tensor')
- feed_down_gradient: float32 [2048, 768], P('tensor', 'dp')
Inputs may be any that keep to these rules, and one draw needn't show every extreme that they name: `decoder_docs`: along each sequence the ids never fall; every sequence holds each of the ids 0, 1, 2, 3, each over 64 tokens or more. Decoder document d of a sequence reads encoder document d of the same sequence. `encoder_docs`: along each sequence the ids never fall; every sequence holds each of the ids 0, 1, 2, 3, each over 32 states or more.
All inputs are finite; a program needn't handle non-finite values.
Results may differ from a plain program's by a relative error of at most 0.023.
The roundings to bfloat16 on the way count: a program that leaves them out, or rounds other values in their place, can miss the bound.
Values may be sent and summed in bfloat16 or wider, within the bound.
A program may use at most 128 MiB of HBM per device.

v0:
```python
import math

import jax
import jax.numpy as jnp
from jax import lax
from jax.sharding import PartitionSpec as P

HEADS = 12
HEAD_DIM = 64
BUCKETS = 32
LEN = 1024


EPS = 1e-06
NEG = -1e30
far_distance = 128


def bucket_edges():
    half = BUCKETS // 2
    upper = [
        int(math.ceil(half * (far_distance / half) ** (step / half)))
        for step in range(1, BUCKETS - half)
    ]
    return list(range(1, half + 1)) + upper


def distance_buckets(distance):
    count = jnp.zeros(distance.shape, jnp.int32)
    for edge in bucket_edges():
        count = count + (distance >= edge).astype(jnp.int32)
    return count


def norm_rows(token_rows, gain):
    return token_rows * lax.rsqrt(jnp.mean(token_rows * token_rows, -1, keepdims=True) + EPS) * gain


def geglu(gate_activation, up_projection_output):
    return jax.nn.gelu(gate_activation, approximate=True) * up_projection_output


def block_bias(table, first, token_rows, keys):
    span = token_rows + keys - 1
    offsets = first + token_rows - 1 - jnp.arange(span, dtype=jnp.int32)
    buckets = distance_buckets(jnp.maximum(offsets, 0))
    onehot = (buckets[:, None] == jnp.arange(table.shape[0], dtype=jnp.int32)[None, :]).astype(
        jnp.float32
    )
    diagonal = jnp.dot(onehot, table, precision=lax.Precision.HIGHEST).T
    padded = jnp.pad(diagonal, ((0, 0), (0, 1)))
    tiled = jnp.tile(padded, (1, token_rows))
    window = lax.slice_in_dim(tiled, token_rows - 1, token_rows - 1 + token_rows * span, axis=1)
    return window.reshape(table.shape[1], token_rows, span)[:, :, :keys]


def causal_mask(docs):
    places = jnp.arange(docs.shape[0], dtype=jnp.int32)

    def allowed(first, token_rows):
        mine = lax.dynamic_slice_in_dim(docs, first, token_rows, 0)
        row_places = first + jnp.arange(token_rows, dtype=jnp.int32)
        return (mine[:, None] == docs[None, :]) & (row_places[:, None] >= places[None, :])

    return allowed


def cross_mask(docs, other_docs):

    def allowed(first, token_rows):
        mine = lax.dynamic_slice_in_dim(docs, first, token_rows, 0)
        return mine[:, None] == other_docs[None, :]

    return allowed


def no_bias(first, token_rows):
    return 0.0


def no_bias_back(first, token_rows, score_grad):
    return jnp.zeros((), jnp.float32)


def block_scores(part, key_heads, allowed, bias, first, token_rows):
    scores = jnp.einsum("qhd,khd->hqk", part, key_heads, preferred_element_type=jnp.float32)
    return jnp.where(allowed(first, token_rows)[None], scores + bias(first, token_rows), NEG)


def attend(query, keys, values, allowed, bias):
    heads = query.shape[1] // HEAD_DIM
    token_rows = min(512, query.shape[0])
    key_heads = keys.reshape(keys.shape[0], heads, HEAD_DIM)
    value_heads = values.reshape(values.shape[0], heads, HEAD_DIM)

    def one_block(first):
        part = lax.dynamic_slice_in_dim(query, first, token_rows, 0).reshape(
            token_rows, heads, HEAD_DIM
        )
        scores = block_scores(part, key_heads, allowed, bias, first, token_rows)
        top = jnp.max(scores, -1, keepdims=True)
        lifted = jnp.exp(scores - top)
        total = jnp.sum(lifted, -1, keepdims=True)
        shares = (lifted / total).astype(jnp.bfloat16)
        mixed = jnp.einsum("hqk,khd->qhd", shares, value_heads, preferred_element_type=jnp.float32)
        return (
            mixed.reshape(token_rows, heads * HEAD_DIM).astype(jnp.bfloat16),
            (top + jnp.log(total))[..., 0],
        )

    starts = jnp.arange(query.shape[0] // token_rows, dtype=jnp.int32) * token_rows
    mixed, log_total = lax.map(one_block, starts)
    return (mixed.reshape(query.shape[0], heads * HEAD_DIM), log_total)


def attend_back(query, keys, values, log_total, mixed_grad, allowed, bias, bias_back, table_zero):
    heads = query.shape[1] // HEAD_DIM
    token_rows = min(512, query.shape[0])
    key_heads = keys.reshape(keys.shape[0], heads, HEAD_DIM)
    value_heads = values.reshape(values.shape[0], heads, HEAD_DIM)

    def one_block(carry, block):
        key_grad, value_grad, table_grad = carry
        first = block * token_rows
        part = lax.dynamic_slice_in_dim(query, first, token_rows, 0).reshape(
            token_rows, heads, HEAD_DIM
        )
        grad_part = lax.dynamic_slice_in_dim(mixed_grad, first, token_rows, 0).reshape(
            token_rows, heads, HEAD_DIM
        )
        scores = block_scores(part, key_heads, allowed, bias, first, token_rows)
        shares = jnp.exp(scores - log_total[block][..., None])
        share_grad = jnp.einsum(
            "qhd,khd->hqk", grad_part, value_heads, preferred_element_type=jnp.float32
        )
        inner = jnp.sum(shares * share_grad, -1, keepdims=True)
        score_grad = shares * (share_grad - inner)
        table_grad = table_grad + bias_back(first, token_rows, score_grad)
        value_grad = value_grad + jnp.einsum(
            "hqk,qhd->khd",
            shares.astype(jnp.bfloat16),
            grad_part,
            preferred_element_type=jnp.float32,
        )
        low_grad = score_grad.astype(jnp.bfloat16)
        query_grad = jnp.einsum(
            "hqk,khd->qhd", low_grad, key_heads, preferred_element_type=jnp.float32
        )
        key_grad = key_grad + jnp.einsum(
            "hqk,qhd->khd", low_grad, part, preferred_element_type=jnp.float32
        )
        return (
            (key_grad, value_grad, table_grad),
            query_grad.reshape(token_rows, heads * HEAD_DIM).astype(jnp.bfloat16),
        )

    zeros = jnp.zeros(key_heads.shape, jnp.float32)
    blocks = jnp.arange(query.shape[0] // token_rows, dtype=jnp.int32)
    (key_grad, value_grad, table_grad), query_grad = lax.scan(
        one_block, (zeros, zeros, table_zero), blocks
    )
    return (
        query_grad.reshape(query.shape),
        key_grad.reshape(keys.shape).astype(jnp.bfloat16),
        value_grad.reshape(values.shape).astype(jnp.bfloat16),
        table_grad,
    )


def gather_rows(value):
    return lax.all_gather(value, "tensor", axis=1, tiled=True)


def scatter_rows(value):
    return lax.psum_scatter(value, "tensor", scatter_dimension=1, tiled=True)


def project(token_rows, weight_matrix):
    return jnp.einsum(
        "vha,am->vhm", token_rows, weight_matrix, preferred_element_type=jnp.float32
    ).astype(jnp.bfloat16)


def weight_product(token_rows, gradient_bundle):
    return jnp.einsum(
        "zpu,zpa->ua", token_rows, gradient_bundle, preferred_element_type=jnp.float32
    )


def back_product(gradient_bundle, weight_matrix):
    return jnp.einsum(
        "vtk,pk->vtp", gradient_bundle, weight_matrix, preferred_element_type=jnp.float32
    )


def on_device(
    states,
    encoder,
    upstream,
    decoder_docs,
    encoder_docs,
    norm_self,
    norm_cross,
    norm_feed,
    position_table,
    self_query,
    self_key,
    self_value,
    self_output,
    cross_query,
    cross_key,
    cross_value,
    cross_output,
    feed_gate,
    feed_up,
    feed_down,
):
    gathered = (
        lax.all_gather(self_query, "dp", axis=0, tiled=True),
        lax.all_gather(self_key, "dp", axis=0, tiled=True),
        lax.all_gather(self_value, "dp", axis=0, tiled=True),
        lax.all_gather(self_output, "dp", axis=1, tiled=True),
        lax.all_gather(cross_query, "dp", axis=0, tiled=True),
        lax.all_gather(cross_key, "dp", axis=0, tiled=True),
        lax.all_gather(cross_value, "dp", axis=0, tiled=True),
        lax.all_gather(cross_output, "dp", axis=1, tiled=True),
        lax.all_gather(feed_gate, "dp", axis=0, tiled=True),
        lax.all_gather(feed_up, "dp", axis=0, tiled=True),
        lax.all_gather(feed_down, "dp", axis=1, tiled=True),
    )
    (
        query_self,
        key_self,
        value_self,
        self_sublayer_output,
        query_cross,
        key_cross,
        value_cross,
        cross_sublayer_output,
        gate_local,
        up_local,
        down_local,
    ) = gathered
    heads = query_self.shape[1] // HEAD_DIM
    tensor_index = lax.axis_index("tensor")
    table_local = lax.dynamic_slice_in_dim(position_table, tensor_index * heads, heads, 1)

    def self_bias(first, token_rows):
        return block_bias(table_local, first, token_rows, LEN)

    def self_bias_back(first, token_rows, score_grad):
        pullback = jax.vjp(lambda table: block_bias(table, first, token_rows, LEN), table_local)[1]
        return pullback(score_grad)[0]

    residual = states.astype(jnp.float32)
    normed, norm_self_back = jax.vjp(norm_rows, residual, norm_self)
    whole_self = gather_rows(normed.astype(jnp.bfloat16))
    queries = project(whole_self, query_self)
    keys = project(whole_self, key_self)
    values = project(whole_self, value_self)

    def self_forward(items):
        return attend(items[0], items[1], items[2], causal_mask(items[3]), self_bias)

    self_attention_blend, self_log = lax.map(self_forward, (queries, keys, values, decoder_docs))
    residual_one = residual + scatter_rows(
        jnp.einsum(
            "hxr,rn->hxn",
            self_attention_blend,
            self_sublayer_output,
            preferred_element_type=jnp.float32,
        )
    )
    normed, norm_cross_back = jax.vjp(norm_rows, residual_one, norm_cross)
    whole_cross = gather_rows(normed.astype(jnp.bfloat16))
    encoder_whole = lax.all_gather(encoder, "tensor", axis=1, tiled=True)
    cross_queries = project(whole_cross, query_cross)
    cross_keys = project(encoder_whole, key_cross)
    cross_values = project(encoder_whole, value_cross)

    def cross_forward(items):
        return attend(items[0], items[1], items[2], cross_mask(items[3], items[4]), no_bias)

    cross_attention_blend, cross_log = lax.map(
        cross_forward, (cross_queries, cross_keys, cross_values, decoder_docs, encoder_docs)
    )
    residual_two = residual_one + scatter_rows(
        jnp.einsum(
            "hxr,rn->hxn",
            cross_attention_blend,
            cross_sublayer_output,
            preferred_element_type=jnp.float32,
        )
    )
    normed, norm_feed_back = jax.vjp(norm_rows, residual_two, norm_feed)
    normed = normed.astype(jnp.bfloat16)
    feedforward_rows = gather_rows(normed)
    gate_weight_applied, up_weight_applied, down_weight_applied = (gate_local, up_local, down_local)
    gate_activation = jnp.einsum(
        "gxo,ow->gxw", feedforward_rows, gate_weight_applied, preferred_element_type=jnp.float32
    )
    up_projection_output = jnp.einsum(
        "gxo,ow->gxw", feedforward_rows, up_weight_applied, preferred_element_type=jnp.float32
    )
    hidden_state, geglu_back = jax.vjp(geglu, gate_activation, up_projection_output)
    hidden_state = hidden_state.astype(jnp.bfloat16)
    feedforward_residual = jnp.einsum(
        "miu,ua->mia", hidden_state, down_weight_applied, preferred_element_type=jnp.float32
    )
    feed_out = scatter_rows(feedforward_residual)
    feedforward_upper_input = gather_rows(upstream)
    layer_output = (residual_two + feed_out).astype(jnp.bfloat16)
    grad_three = upstream.astype(jnp.float32)
    feed_down_gradient = jnp.einsum(
        "awy,awo->yo", hidden_state, feedforward_upper_input, preferred_element_type=jnp.float32
    )
    hidden_state_gradient = jnp.einsum(
        "ice,te->ict",
        feedforward_upper_input,
        down_weight_applied,
        preferred_element_type=jnp.float32,
    )
    gate_grad, up_grad = geglu_back(hidden_state_gradient)
    gate_grad = gate_grad.astype(jnp.bfloat16)
    up_grad = up_grad.astype(jnp.bfloat16)
    feed_gate_gradient = weight_product(feedforward_rows, gate_grad)
    feed_up_gradient = weight_product(feedforward_rows, up_grad)
    rows_grad = back_product(gate_grad, gate_weight_applied) + back_product(
        up_grad, up_weight_applied
    )
    feed_grad = scatter_rows(rows_grad)
    step_grad, norm_feed_gradient = norm_feed_back(feed_grad)
    grad_two = grad_three + step_grad
    cross_upper_input = gather_rows(grad_two.astype(jnp.bfloat16))
    cross_output_gradient = jnp.einsum(
        "bgv,bgt->vt", cross_attention_blend, cross_upper_input, preferred_element_type=jnp.float32
    )
    cross_mixed_grad = jnp.einsum(
        "qik,hk->qih", cross_upper_input, cross_sublayer_output, preferred_element_type=jnp.float32
    ).astype(jnp.bfloat16)

    def cross_backward(items):
        return attend_back(
            items[0],
            items[1],
            items[2],
            items[3],
            items[4],
            cross_mask(items[5], items[6]),
            no_bias,
            no_bias_back,
            jnp.zeros((), jnp.float32),
        )

    cross_query_rows, cross_key_rows, cross_value_rows, unused = lax.map(
        cross_backward,
        (
            cross_queries,
            cross_keys,
            cross_values,
            cross_log,
            cross_mixed_grad,
            decoder_docs,
            encoder_docs,
        ),
    )
    cross_query_gradient = weight_product(whole_cross, cross_query_rows)
    cross_key_gradient = weight_product(encoder_whole, cross_key_rows)
    cross_value_gradient = weight_product(encoder_whole, cross_value_rows)
    encoder_part = back_product(cross_key_rows, key_cross) + back_product(
        cross_value_rows, value_cross
    )
    encoder_gradient = lax.psum_scatter(
        encoder_part.astype(jnp.bfloat16), "tensor", scatter_dimension=1, tiled=True
    ).astype(jnp.float32)
    step_grad, norm_cross_gradient = norm_cross_back(
        scatter_rows(back_product(cross_query_rows, query_cross))
    )
    grad_one = grad_two + step_grad
    self_upper_input = gather_rows(grad_one.astype(jnp.bfloat16))
    self_output_gradient = jnp.einsum(
        "bgv,bgt->vt", self_attention_blend, self_upper_input, preferred_element_type=jnp.float32
    )
    self_mixed_grad = jnp.einsum(
        "qik,hk->qih", self_upper_input, self_sublayer_output, preferred_element_type=jnp.float32
    ).astype(jnp.bfloat16)

    def self_backward(items):
        return attend_back(
            items[0],
            items[1],
            items[2],
            items[3],
            items[4],
            causal_mask(items[5]),
            self_bias,
            self_bias_back,
            jnp.zeros(table_local.shape, jnp.float32),
        )

    query_rows, key_rows, value_rows, table_parts = lax.map(
        self_backward, (queries, keys, values, self_log, self_mixed_grad, decoder_docs)
    )
    self_query_gradient = weight_product(whole_self, query_rows)
    self_key_gradient = weight_product(whole_self, key_rows)
    self_value_gradient = weight_product(whole_self, value_rows)
    normed_grad = (
        back_product(query_rows, query_self)
        + back_product(key_rows, key_self)
        + back_product(value_rows, value_self)
    )
    step_grad, norm_self_gradient = norm_self_back(scatter_rows(normed_grad))
    states_gradient = grad_one + step_grad
    weight_gradients = (
        lax.psum_scatter(self_query_gradient, "dp", scatter_dimension=0, tiled=True),
        lax.psum_scatter(self_key_gradient, "dp", scatter_dimension=0, tiled=True),
        lax.psum_scatter(self_value_gradient, "dp", scatter_dimension=0, tiled=True),
        lax.psum_scatter(self_output_gradient, "dp", scatter_dimension=1, tiled=True),
        lax.psum_scatter(cross_query_gradient, "dp", scatter_dimension=0, tiled=True),
        lax.psum_scatter(cross_key_gradient, "dp", scatter_dimension=0, tiled=True),
        lax.psum_scatter(cross_value_gradient, "dp", scatter_dimension=0, tiled=True),
        lax.psum_scatter(cross_output_gradient, "dp", scatter_dimension=1, tiled=True),
        lax.psum_scatter(feed_gate_gradient, "dp", scatter_dimension=0, tiled=True),
        lax.psum_scatter(feed_up_gradient, "dp", scatter_dimension=0, tiled=True),
        lax.psum_scatter(feed_down_gradient, "dp", scatter_dimension=1, tiled=True),
    )
    table_full = lax.dynamic_update_slice_in_dim(
        jnp.zeros((BUCKETS, HEADS), jnp.float32), jnp.sum(table_parts, 0), tensor_index * heads, 1
    )
    norm_self_gradient, norm_cross_gradient, norm_feed_gradient, table_gradient = lax.psum(
        (norm_self_gradient, norm_cross_gradient, norm_feed_gradient, table_full), ("dp", "tensor")
    )
    return (
        layer_output,
        states_gradient,
        encoder_gradient,
        norm_self_gradient,
        norm_cross_gradient,
        norm_feed_gradient,
        table_gradient,
        weight_gradients[0],
        weight_gradients[1],
        weight_gradients[2],
        weight_gradients[3],
        weight_gradients[4],
        weight_gradients[5],
        weight_gradients[6],
        weight_gradients[7],
        weight_gradients[8],
        weight_gradients[9],
        weight_gradients[10],
    )


def solution(mesh):
    return jax.shard_map(
        on_device,
        mesh=mesh,
        in_specs=(
            P("dp", "tensor", None),
            P("dp", "tensor", None),
            P("dp", "tensor", None),
            P("dp", None),
            P("dp", None),
            P(),
            P(),
            P(),
            P(),
            P("dp", "tensor"),
            P("dp", "tensor"),
            P("dp", "tensor"),
            P("tensor", "dp"),
            P("dp", "tensor"),
            P("dp", "tensor"),
            P("dp", "tensor"),
            P("tensor", "dp"),
            P("dp", "tensor"),
            P("dp", "tensor"),
            P("tensor", "dp"),
        ),
        out_specs=(
            P("dp", "tensor", None),
            P("dp", "tensor", None),
            P("dp", "tensor", None),
            P(),
            P(),
            P(),
            P(),
            P("dp", "tensor"),
            P("dp", "tensor"),
            P("dp", "tensor"),
            P("tensor", "dp"),
            P("dp", "tensor"),
            P("dp", "tensor"),
            P("dp", "tensor"),
            P("tensor", "dp"),
            P("dp", "tensor"),
            P("dp", "tensor"),
            P("tensor", "dp"),
        ),
        check_vma=False,
    )
```

profile of v0, /device:TPU:0, one launch (start us, length us, event | category | flops | bytes accessed | tf_op | source)
XLA Modules:
  0.0 1792.0 jit_solution(11391979746343091043)
XLA Ops:
  12.5 34.9 %all_gather.58 = bf16[192,768]{0,1:T(8,128)(2,1)} all-gather(bf16[192,96]{0,1:T(8,128)(2,1)S(1)} %copy.59), channel_id=1, replica_groups=mesh['dp'=8,'tensor'=4] {'dp'}, dimensions={1}, use_global_device_ids=true | all-gather | bytes 331776 | tf_op jit(solution)/shard_map/all_gather | solution.py:222
  47.4 31.5 %all_gather.55 = bf16[768,192]{1,0:T(8,128)(2,1)S(1)} all-gather(bf16[96,192]{1,0:T(8,128)(2,1)} %param.37), channel_id=1, replica_groups=mesh['dp'=8,'tensor'=4] {'dp'}, dimensions={0}, use_global_device_ids=true | all-gather | bytes 331776 | tf_op jit(solution)/shard_map/all_gather | solution.py:219
  78.9 31.4 %all_gather.56 = bf16[768,192]{1,0:T(8,128)(2,1)S(1)} all-gather(bf16[96,192]{1,0:T(8,128)(2,1)} %param.38), channel_id=1, replica_groups=mesh['dp'=8,'tensor'=4] {'dp'}, dimensions={0}, use_global_device_ids=true | all-gather | bytes 331776 | tf_op jit(solution)/shard_map/all_gather | solution.py:220
  146.6 143.7 %while.108 = (s32[]{:T(128)}, bf16[2,512,192]{1,2,0:T(8,128)(2,1)S(1)}, f32[2,3,512]{2,1,0:T(4,128)S(1)}, s32[2]{0:T(128)S(1)}, s32[1024]{0:T(1024)S(1)}, /*inde...) while((s32[]{:T(128)}, ...), condition=%wide.region_4.5_spmd.clone, body=%wide.region_1.4_spmd.clone.sunk | while | flops 418867968 | bytes 113234472 | solution.py:112
  292.8 38.8 %reduce-scatter.27.cloned.1.call-done = f32[1,256,768]{2,1,0:T(8,128)} async-done(((f32[1,1024,768]{2,1,0:T(8,128)}), f32[1,256,768]{2,1,0:T(8,128)}) %reduce-scatter.27.cloned.1.call-update) | async-done | bytes 786448 | tf_op jit(solution)/shard_map/reduce_scatter | solution.py:175
  334.0 33.2 %all_gather.64 = bf16[192,768]{0,1:T(8,128)(2,1)} all-gather(bf16[192,96]{0,1:T(8,128)(2,1)S(1)} %copy.61), channel_id=1, replica_groups=mesh['dp'=8,'tensor'=4] {'dp'}, dimensions={1}, use_global_device_ids=true | all-gather | bytes 331776 | tf_op jit(solution)/shard_map/all_gather | solution.py:226
  367.2 33.1 %all_gather.60 = bf16[768,192]{1,0:T(8,128)(2,1)} all-gather(bf16[96,192]{1,0:T(8,128)(2,1)S(1)} %copy-done.66), channel_id=1, replica_groups=mesh['dp'=8,'tensor'=4] {'dp'}, dimensions={0}, use_global_device_ids=true | all-gather | bytes 331776 | tf_op jit(solution)/shard_map/all_gather | solution.py:223
  488.3 39.4 %reduce-scatter.29.cloned.1.call-done = f32[1,256,768]{2,1,0:T(8,128)} async-done(((f32[1,1024,768]{2,1,0:T(8,128)}), f32[1,256,768]{2,1,0:T(8,128)}) %reduce-scatter.29.cloned.1.call-update) | async-done | bytes 786448 | tf_op jit(solution)/shard_map/reduce_scatter | solution.py:175
  530.6 34.3 %all_gather.66 = bf16[768,512]{1,0:T(8,128)(2,1)} all-gather(bf16[96,512]{1,0:T(8,128)(2,1)S(1)} %copy-done.62), channel_id=1, replica_groups=mesh['dp'=8,'tensor'=4] {'dp'}, dimensions={0}, use_global_device_ids=true | all-gather | bytes 884736 | tf_op jit(solution)/shard_map/all_gather | solution.py:227
  564.9 34.0 %all_gather.67 = bf16[768,512]{1,0:T(8,128)(2,1)} all-gather(bf16[96,512]{1,0:T(8,128)(2,1)S(1)} %copy-done.63), channel_id=1, replica_groups=mesh['dp'=8,'tensor'=4] {'dp'}, dimensions={0}, use_global_device_ids=true | all-gather | bytes 884736 | tf_op jit(solution)/shard_map/all_gather | solution.py:228
  598.9 34.3 %all_gather.68 = bf16[512,768]{0,1:T(8,128)(2,1)} all-gather(bf16[512,96]{0,1:T(8,128)(2,1)S(1)} %copy-done.64), channel_id=1, replica_groups=mesh['dp'=8,'tensor'=4] {'dp'}, dimensions={1}, use_global_device_ids=true | all-gather | bytes 884736 | tf_op jit(solution)/shard_map/all_gather | solution.py:229
  650.8 37.9 %reduce-scatter.33.cloned.1.call-done = f32[1,256,768]{2,1,0:T(8,128)} async-done(((f32[1,1024,768]{2,1,0:T(8,128)}), f32[1,256,768]{2,1,0:T(8,128)}) %reduce-scatter.33.cloned.1.call-update) | async-done | bytes 786448 | tf_op jit(solution)/shard_map/reduce_scatter | solution.py:175
  745.7 33.8 %reduce-scatter.35.cloned.1.call-done = f32[1,256,768]{2,1,0:T(8,128)} async-done(((f32[1,1024,768]{2,1,0:T(8,128)}), f32[1,256,768]{2,1,0:T(8,128)}) %reduce-scatter.35.cloned.1.call-update) | async-done | bytes 786448 | tf_op jit(solution)/shard_map/reduce_scatter | solution.py:175
  781.5 38.4 %reduce-scatter.31.cloned.1.call-done = f32[1,256,768]{2,1,0:T(8,128)} async-done(((f32[1,1024,768]{2,1,0:T(8,128)}), f32[1,256,768]{2,1,0:T(8,128)}) %reduce-scatter.31.cloned.1.call-update) | async-done | bytes 786448 | tf_op jit(solution)/shard_map/reduce_scatter | solution.py:175
  848.5 292.8 %while.110 = (s32[]{:T(128)}, f32[1024,3,64]{0,2,1:T(8,128)}, f32[1024,3,64]{0,2,1:T(8,128)}, f32[32,3]{0,1:T(4,128)S(1)}, bf16[2,512,192]{1,2,0:T(8,128)(2,1)},...) while((s32[]{:T(128)}, f32[1024,3,64]{0,2,1:T(8,128)}, ...), condition=%wide.region_24.25_spmd.clone, body=%wide.region_21.24_spmd.clone.sunk | while | flops 1030952192 | bytes 276598496 | solution.py:159
  1188.3 40.3 %all-reduce.4 = (f32[768]{0:T(1024)}, f32[768]{0:T(1024)}, f32[768]{0:T(1024)}, f32[32,12]{0,1:T(8,128)}) all-reduce(f32[768]{0:T(1024)S(1)} %get-tuple-element.897, f32[768]{0:T(1024)S(1)} %copy-done.75, f32[768]{0:T(1024)S(1)} %copy-done.74, f32[32,12]{0,1:T(8,128)S(1)} %dynamic_update_slice.67), channel_id=1, replica_groups=mesh['dp'=8,'tensor'=4] {'dp','tensor'}, use_global_device_ids=true, to_apply=%region_29.30 | all-reduce | flops 2688 | bytes 21504 | tf_op jit(solution)/shard_map/psum | solution.py:430
  1256.3 67.6 %reduce-scatter.49.cloned.1.call-done = f32[96,512]{1,0:T(8,128)} async-done(((f32[768,512]{1,0:T(8,128)}), f32[96,512]{1,0:T(8,128)}) %reduce-scatter.49.cloned.1.call-update) | async-done | bytes 196624 | tf_op jit(solution)/shard_map/reduce_scatter | solution.py:423
  1323.9 68.0 %reduce-scatter.51.cloned.1.call-done = f32[96,512]{1,0:T(8,128)} async-done(((f32[768,512]{1,0:T(8,128)}), f32[96,512]{1,0:T(8,128)}) %reduce-scatter.51.cloned.1.call-update) | async-done | bytes 196624 | tf_op jit(solution)/shard_map/reduce_scatter | solution.py:424
  1391.9 65.3 %reduce-scatter.47.cloned.1.call-done = f32[96,192]{1,0:T(8,128)} async-done(((f32[768,192]{1,0:T(8,128)}), f32[96,192]{1,0:T(8,128)}) %reduce-scatter.47.cloned.1.call-update) | async-done | bytes 73744 | tf_op jit(solution)/shard_map/reduce_scatter | solution.py:419
  1457.2 65.6 %reduce-scatter.57.cloned.1.call-done = f32[96,192]{1,0:T(8,128)} async-done(((f32[768,192]{1,0:T(8,128)}), f32[96,192]{1,0:T(8,128)}) %reduce-scatter.57.cloned.1.call-update) | async-done | bytes 73744
  1522.8 65.4 %reduce-scatter.59.cloned.1.call-done = f32[96,192]{1,0:T(8,128)} async-done(((f32[768,192]{1,0:T(8,128)}), f32[96,192]{1,0:T(8,128)}) %reduce-scatter.59.cloned.1.call-update) | async-done | bytes 73744
  1588.2 65.8 %reduce-scatter.45.cloned.1.call-done = f32[96,192]{1,0:T(8,128)} async-done(((f32[768,192]{1,0:T(8,128)}), f32[96,192]{1,0:T(8,128)}) %reduce-scatter.45.cloned.1.call-update) | async-done | bytes 73744 | tf_op jit(solution)/shard_map/reduce_scatter | solution.py:417
  1654.0 65.4 %reduce-scatter.41.cloned.1.call-done = f32[96,192]{1,0:T(8,128)} async-done(((f32[768,192]{1,0:T(8,128)}), f32[96,192]{1,0:T(8,128)}) %reduce-scatter.41.cloned.1.call-update) | async-done | bytes 73744 | tf_op jit(solution)/shard_map/reduce_scatter | solution.py:415
  1719.3 65.6 %reduce-scatter.43.cloned.1.call-done = f32[96,192]{1,0:T(8,128)} async-done(((f32[768,192]{1,0:T(8,128)}), f32[96,192]{1,0:T(8,128)}) %reduce-scatter.43.cloned.1.call-update) | async-done | bytes 73744 | tf_op jit(solution)/shard_map/reduce_scatter | solution.py:416
  (476 shorter events, 732.9 us)
Async XLA Ops:
  7.2 134.2 %all-gather.7.cloned.1.call-start = ((), (), s32[]{:S(2)}) async-start(), calls=%async_computation.18 | async-start | bytes 1966080 | tf_op jit(solution)/shard_map/all_gather | solution.py:171
  11.5 320.1 %reduce-scatter.27.cloned.1.call-start = ((), (), s32[]{:S(2)}) async-start(), calls=%async_computation.19 | async-start | bytes 3932160 | tf_op jit(solution)/shard_map/reduce_scatter | solution.py:175
  292.7 178.5 %all-gather.9.cloned.1.call-start = ((), (), s32[]{:S(2)}) async-start(), calls=%async_computation.20 | async-start | bytes 1966080 | tf_op jit(solution)/shard_map/all_gather | solution.py:171
  333.8 193.9 %reduce-scatter.29.cloned.1.call-start = ((), (), s32[]{:S(2)}) async-start(), calls=%async_computation.21 | async-start | bytes 3932160 | tf_op jit(solution)/shard_map/reduce_scatter | solution.py:175
  488.2 145.0 %all-gather.11.cloned.1.call-start = ((), (), s32[]{:S(2)}) async-start(), calls=%async_computation.22 | async-start | bytes 1966080 | tf_op jit(solution)/shard_map/all_gather | solution.py:171
  530.0 109.7 %all-gather.13.cloned.1.call-start = ((), (), s32[]{:S(2)}) async-start(), calls=%async_computation.24 | async-start | bytes 1966080 | tf_op jit(solution)/shard_map/all_gather | solution.py:171
  530.5 158.2 %reduce-scatter.33.cloned.1.call-start = ((), (), s32[]{:S(2)}) async-start(), calls=%async_computation.25 | async-start | bytes 3932160 | tf_op jit(solution)/shard_map/reduce_scatter | solution.py:175
  650.4 62.3 %all-gather.15.cloned.1.call-start = ((), (), s32[]{:S(2)}) async-start(), calls=%async_computation.26 | async-start | bytes 1966080 | tf_op jit(solution)/shard_map/all_gather | solution.py:171
  692.9 86.6 %reduce-scatter.35.cloned.1.call-start = ((), (), s32[]{:S(2)}) async-start(), calls=%async_computation.27 | async-start | bytes 3932160 | tf_op jit(solution)/shard_map/reduce_scatter | solution.py:175
  741.5 78.4 %reduce-scatter.31.cloned.1.call-start = ((), (), s32[]{:S(2)}) async-start(), calls=%async_computation.23 | async-start | bytes 3932160 | tf_op jit(solution)/shard_map/reduce_scatter | solution.py:175
  745.7 97.3 %all-gather.17.cloned.1.call-start = ((), (), s32[]{:S(2)}) async-start(), calls=%async_computation.28 | async-start | bytes 1966080 | tf_op jit(solution)/shard_map/all_gather | solution.py:171
  823.1 353.4 %reduce-scatter.61.cloned.1.call-start = ((), (), s32[]{:S(2)}) async-start(), calls=%async_computation.41 | async-start | bytes 884736
  826.4 351.7 %reduce-scatter.39.cloned.1.call-start = ((), (), s32[]{:S(2)}) async-start(), calls=%async_computation.30 | async-start | bytes 983040 | tf_op jit(solution)/shard_map/reduce_scatter | solution.py:373
  830.5 349.5 %reduce-scatter.55.cloned.1.call-start = ((), (), s32[]{:S(2)}) async-start(), calls=%async_computation.38 | async-start | bytes 884736
  846.2 340.6 %reduce-scatter.37.cloned.1.call-start = ((), (), s32[]{:S(2)}) async-start(), calls=%async_computation.29 | async-start | bytes 3932160 | tf_op jit(solution)/shard_map/reduce_scatter | solution.py:175
  1148.7 107.6 %reduce-scatter.53.cloned.1.call-start = ((), (), s32[]{:S(2)}) async-start(), calls=%async_computation.37 | async-start | bytes 1769472 | tf_op jit(solution)/shard_map/reduce_scatter | solution.py:425
  1153.5 170.4 %reduce-scatter.49.cloned.1.call-start = ((), (), s32[]{:S(2)}) async-start(), calls=%async_computation.35 | async-start | bytes 1769472 | tf_op jit(solution)/shard_map/reduce_scatter | solution.py:423
  1157.5 234.4 %reduce-scatter.51.cloned.1.call-start = ((), (), s32[]{:S(2)}) async-start(), calls=%async_computation.36 | async-start | bytes 1769472 | tf_op jit(solution)/shard_map/reduce_scatter | solution.py:424
  1161.8 295.4 %reduce-scatter.47.cloned.1.call-start = ((), (), s32[]{:S(2)}) async-start(), calls=%async_computation.34 | async-start | bytes 884736 | tf_op jit(solution)/shard_map/reduce_scatter | solution.py:419
  1163.4 359.4 %reduce-scatter.57.cloned.1.call-start = ((), (), s32[]{:S(2)}) async-start(), calls=%async_computation.39 | async-start | bytes 884736
  1168.0 420.1 %reduce-scatter.59.cloned.1.call-start = ((), (), s32[]{:S(2)}) async-start(), calls=%async_computation.40 | async-start | bytes 884736
  1171.5 482.4 %reduce-scatter.45.cloned.1.call-start = ((), (), s32[]{:S(2)}) async-start(), calls=%async_computation.33 | async-start | bytes 884736 | tf_op jit(solution)/shard_map/reduce_scatter | solution.py:417
  1173.2 546.2 %reduce-scatter.41.cloned.1.call-start = ((), (), s32[]{:S(2)}) async-start(), calls=%async_computation.31 | async-start | bytes 884736 | tf_op jit(solution)/shard_map/reduce_scatter | solution.py:415
  1174.8 610.1 %reduce-scatter.43.cloned.1.call-start = ((), (), s32[]{:S(2)}) async-start(), calls=%async_computation.32 | async-start | bytes 884736 | tf_op jit(solution)/shard_map/reduce_scatter | solution.py:416
  (97 other events, 2371.6 us)
Sparse Core Ops, SparseCore 0:
  11.6 22.3 all-gather.6
  292.8 38.7 reduce-scatter.26
  334.0 19.6 all-gather.8
  488.3 39.3 reduce-scatter.28
  530.1 19.6 all-gather.10
  551.2 19.6 all-gather.12
  650.6 38.1 reduce-scatter.32
  693.0 19.6 all-gather.14
  741.6 37.9 reduce-scatter.34
  781.9 37.9 reduce-scatter.30
  823.2 19.6 all-gather.16
  846.5 62.4 reduce-scatter.60
  911.5 22.2 reduce-scatter.38
  937.3 62.5 reduce-scatter.54
  1148.8 38.0 reduce-scatter.36
  1191.1 65.1 reduce-scatter.52
  1260.1 63.7 reduce-scatter.48
  1328.1 63.7 reduce-scatter.50
  1395.8 61.4 reduce-scatter.46
  1461.3 61.4 reduce-scatter.56
  1526.7 61.4 reduce-scatter.58
  1592.4 61.5 reduce-scatter.44
  1657.8 61.4 reduce-scatter.40
  1723.4 61.4 reduce-scatter.42
where the time goes:
time: 1800 us; the launch traced here: 1790 us
  waiting for transfers between devices  781 us (43%)
  blocking collectives  408 us (23%)
  local copies, waits for them, and re-layouts  351 us (20%)
  matrix products  136 us (8%)
  loops' own time  50.8 us (3%)
  other arithmetic  48.5 us (3%)
    reduce_scatter x6, waiting for transfers between devices, scatter_rows(): return lax.psum_scatter(value, 'tensor', scatter_dimension=1, tiled=True)  194 us
    while x78, local copies, waits for them, and re-layouts  170 us
    unnamed x28, waiting for transfers between devices  132 us
    reshape x6, local copies, waits for them, and re-layouts, block_bias(): return window.reshape(table.shape[1], token_rows, span)[:, :, :keys]  89.1 us
    reduce_scatter x1, waiting for transfers between devices, on_device(): lax.psum_scatter(feed_up_gradient, 'dp', scatter_dimension=0, tiled=True)  68 us
    reduce_scatter x1, waiting for transfers between devices, on_device(): lax.psum_scatter(feed_gate_gradient, 'dp', scatter_dimension=0, tiled=True)  67.6 us
    reduce_scatter x1, waiting for transfers between devices, on_device(): lax.psum_scatter(self_value_gradient, 'dp', scatter_dimension=0, tiled=True)  65.8 us
    reduce_scatter x1, waiting for transfers between devices, on_device(): lax.psum_scatter(self_key_gradient, 'dp', scatter_dimension=0, tiled=True)  65.6 us
  transfers between devices with their start and end apart: 24, of which 17 were waited for; matrix products, arithmetic and copies ran while one was open for 18% of the time, Pallas kernels for 0%

commit v1 on v0

v1 whole, which is shorter than its diff:
```python
import functools
import math

import jax
import jax.numpy as jnp
from jax import lax
from jax.experimental import pallas as pl
from jax.experimental.pallas import tpu as pltpu
from jax.sharding import PartitionSpec as P

HEADS = 12
HEAD_DIM = 64
BUCKETS = 32

EPS = 1e-06
NEG = -1e30
far_distance = 128


def bucket_edges():
    half = BUCKETS // 2
    upper = [
        int(math.ceil(half * (far_distance / half) ** (step / half)))
        for step in range(1, BUCKETS - half)
    ]
    return list(range(1, half + 1)) + upper


def distance_buckets(distance):
    count = jnp.zeros(distance.shape, jnp.int32)
    for edge in bucket_edges():
        count = count + (distance >= edge).astype(jnp.int32)
    return count


def dot(left, right, left_dim, right_dim):
    return lax.dot_general(
        left, right, (((left_dim,), (right_dim,)), ((), ())), preferred_element_type=jnp.float32
    )


def window_distance(shape, window, block):
    place = lax.broadcasted_iota(jnp.int32, shape, len(shape) - 1)
    return jnp.where(place > block, block + window - place, block - place)


def bias_window(table_ref, head, block):
    window = 2 * block
    distance = window_distance((8, window), window, block)
    count = distance_buckets(distance)
    line = jnp.zeros((8, window), jnp.float32)
    for bucket in range(BUCKETS):
        line = jnp.where(count == bucket, table_ref[head, bucket], line)
    row = lax.broadcasted_iota(jnp.int32, (8, window), 0)
    for step in (1, 2, 4):
        line = jnp.where((row & step) != 0, pltpu.roll(line, step, 1), line)
    step = 8
    while step < block:
        line = jnp.concatenate([line, pltpu.roll(line, step, 1)], 0)
        step = 2 * step
    return line


def diagonal_sums(tile, block):
    window = 2 * block
    step = block // 2
    while step >= 8:
        tile = tile[:step] + pltpu.roll(tile[step:], window - step, 1)
        step = step // 2
    row = lax.broadcasted_iota(jnp.int32, (8, window), 0)
    for step in (1, 2, 4):
        tile = jnp.where((row & step) != 0, pltpu.roll(tile, window - step, 1), tile)
    return jnp.sum(tile, 0, keepdims=True)


def self_scores(query, keys, docs_column, docs_row, index, block, table_ref, head, wide):
    size = (index + 1) * block
    raw = dot(query, keys[:size], 1, 1)
    parts = []
    for other in range(index + 1):
        piece = raw[:, other * block : (other + 1) * block]
        if other == index:
            piece = piece + wide[:, block:]
        elif other == index - 1:
            piece = piece + wide[:, :block]
        else:
            piece = piece + table_ref[head, BUCKETS - 1]
        same = docs_column == docs_row[:, other * block : (other + 1) * block]
        if other == index:
            place = lax.broadcasted_iota(jnp.int32, (block, block), 0)
            same = same & (place >= lax.broadcasted_iota(jnp.int32, (block, block), 1))
        parts.append(jnp.where(same, piece, NEG))
    return jnp.concatenate(parts, 1) if len(parts) > 1 else parts[0]


def softmax_mix(scores, values):
    top = jnp.max(scores, -1, keepdims=True)
    lifted = jnp.exp(scores - top)
    total = jnp.sum(lifted, -1, keepdims=True)
    shares = (lifted * (1.0 / total)).astype(jnp.bfloat16)
    return dot(shares, values, 1, 0).astype(jnp.bfloat16), top + jnp.log(total)


def head_slice(head):
    return slice(head * HEAD_DIM, (head + 1) * HEAD_DIM)


def self_forward_kernel(heads, block, table_ref, column_ref, row_ref, qkv_ref, mixed_ref, log_ref):
    width = heads * HEAD_DIM
    length = qkv_ref.shape[1]
    qkv = qkv_ref[0]
    docs_row = row_ref[0]
    mixed_heads, log_heads = [], []
    for head in range(heads):
        wide = bias_window(table_ref, head, block)
        cut = head_slice(head)
        query, keys, values = (
            qkv[:, part * width + cut.start : part * width + cut.stop] for part in range(3)
        )
        mixed_blocks, log_blocks = [], []
        for index in range(length // block):
            rows = slice(index * block, (index + 1) * block)
            scores = self_scores(
                query[rows], keys, column_ref[0, rows], docs_row, index, block, table_ref, head, wide
            )
            mixed, log_total = softmax_mix(scores, values[: rows.stop])
            mixed_blocks.append(mixed)
            log_blocks.append(log_total)
        mixed_heads.append(jnp.concatenate(mixed_blocks, 0))
        log_heads.append(jnp.concatenate(log_blocks, 0))
    mixed_ref[0] = jnp.concatenate(mixed_heads, 1)
    log_ref[0] = jnp.concatenate(log_heads, 1)


def self_backward_kernel(
    heads, block, table_ref, column_ref, row_ref, qkv_ref, log_ref, grad_ref, out_ref, diagonal_ref
):
    width = heads * HEAD_DIM
    length = qkv_ref.shape[1]
    window = 2 * block
    qkv = qkv_ref[0]
    grads = grad_ref[0]
    docs_row = row_ref[0]
    query_heads, key_heads, value_heads = [], [], []
    for head in range(heads):
        wide = bias_window(table_ref, head, block)
        cut = head_slice(head)
        query, keys, values = (
            qkv[:, part * width + cut.start : part * width + cut.stop] for part in range(3)
        )
        grad = grads[:, cut]
        blocks = length // block
        key_sums = [None] * blocks
        value_sums = [None] * blocks
        query_blocks = []
        near = jnp.zeros((block, block), jnp.float32)
        before = jnp.zeros((block, block), jnp.float32)
        far = jnp.zeros((1, block), jnp.float32)
        for index in range(blocks):
            rows = slice(index * block, (index + 1) * block)
            scores = self_scores(
                query[rows], keys, column_ref[0, rows], docs_row, index, block, table_ref, head, wide
            )
            shares = jnp.exp(scores - log_ref[0, rows, head : head + 1])
            share_grad = dot(grad[rows], values[: rows.stop], 1, 1)
            inner = jnp.sum(shares * share_grad, -1, keepdims=True)
            score_grad = shares * (share_grad - inner)
            low = score_grad.astype(jnp.bfloat16)
            query_blocks.append(dot(low, keys[: rows.stop], 1, 0).astype(jnp.bfloat16))
            key_part = dot(low, query[rows], 0, 0)
            value_part = dot(shares.astype(jnp.bfloat16), grad[rows], 0, 0)
            for other in range(index + 1):
                cols = slice(other * block, (other + 1) * block)
                key_sums[other] = (
                    key_part[cols] if key_sums[other] is None else key_sums[other] + key_part[cols]
                )
                value_sums[other] = (
                    value_part[cols]
                    if value_sums[other] is None
                    else value_sums[other] + value_part[cols]
                )
                if other == index:
                    near = near + score_grad[:, cols]
                elif other == index - 1:
                    before = before + score_grad[:, cols]
                else:
                    far = far + jnp.sum(score_grad[:, cols], 0, keepdims=True)
        line = diagonal_sums(jnp.concatenate([before, near], 1), block)
        place = lax.broadcasted_iota(jnp.int32, (1, window), 1)
        line = jnp.where(place == block + 1, line + jnp.sum(far), line)
        diagonal_ref[0, head : head + 1] = line
        query_heads.append(jnp.concatenate(query_blocks, 0))
        key_heads.append(jnp.concatenate(key_sums, 0).astype(jnp.bfloat16))
        value_heads.append(jnp.concatenate(value_sums, 0).astype(jnp.bfloat16))
    out_ref[0] = jnp.concatenate(query_heads + key_heads + value_heads, 1)


def cross_scores(query, keys, docs_column, docs_row):
    return jnp.where(docs_column == docs_row, dot(query, keys, 1, 1), NEG)


def cross_forward_kernel(heads, block, column_ref, row_ref, query_ref, both_ref, mixed_ref, log_ref):
    width = heads * HEAD_DIM
    both = both_ref[0]
    for index in range(query_ref.shape[1] // block):
        rows = slice(index * block, (index + 1) * block)
        mixed_heads, log_heads = [], []
        for head in range(heads):
            cut = head_slice(head)
            scores = cross_scores(
                query_ref[0, rows, cut], both[:, cut], column_ref[0, rows], row_ref[0]
            )
            mixed, log_total = softmax_mix(scores, both[:, width + cut.start : width + cut.stop])
            mixed_heads.append(mixed)
            log_heads.append(log_total)
        mixed_ref[0, rows] = jnp.concatenate(mixed_heads, 1)
        log_ref[0, rows] = jnp.concatenate(log_heads, 1)


def cross_backward_kernel(
    heads, block, column_ref, row_ref, query_ref, both_ref, log_ref, grad_ref, out_ref, both_out_ref
):
    width = heads * HEAD_DIM
    both = both_ref[0]
    query_heads, key_heads, value_heads = [], [], []
    for head in range(heads):
        cut = head_slice(head)
        keys = both[:, cut]
        values = both[:, width + cut.start : width + cut.stop]
        key_sum = value_sum = None
        query_blocks = []
        for index in range(query_ref.shape[1] // block):
            rows = slice(index * block, (index + 1) * block)
            query = query_ref[0, rows, cut]
            grad = grad_ref[0, rows, cut]
            scores = cross_scores(query, keys, column_ref[0, rows], row_ref[0])
            shares = jnp.exp(scores - log_ref[0, rows, head : head + 1])
            share_grad = dot(grad, values, 1, 1)
            inner = jnp.sum(shares * share_grad, -1, keepdims=True)
            low = (shares * (share_grad - inner)).astype(jnp.bfloat16)
            query_blocks.append(dot(low, keys, 1, 0).astype(jnp.bfloat16))
            key_part = dot(low, query, 0, 0)
            value_part = dot(shares.astype(jnp.bfloat16), grad, 0, 0)
            key_sum = key_part if key_sum is None else key_sum + key_part
            value_sum = value_part if value_sum is None else value_sum + value_part
        query_heads.append(jnp.concatenate(query_blocks, 0))
        key_heads.append(key_sum.astype(jnp.bfloat16))
        value_heads.append(value_sum.astype(jnp.bfloat16))
    out_ref[0] = jnp.concatenate(query_heads, 1)
    both_out_ref[0] = jnp.concatenate(key_heads + value_heads, 1)


def whole_block(value):
    shape = (1,) + value.shape[1:]
    return pl.BlockSpec(shape, lambda part: (part,) + (0,) * (len(shape) - 1))


def per_sequence(kernel, table, arrays, outs):
    ins = [whole_block(value) for value in arrays]
    operands = list(arrays)
    if table is not None:
        ins.insert(0, pl.BlockSpec(memory_space=pltpu.SMEM))
        operands.insert(0, table)
    return pl.pallas_call(
        kernel,
        grid=(arrays[0].shape[0],),
        in_specs=ins,
        out_specs=[whole_block(value) for value in outs],
        out_shape=outs,
        compiler_params=pltpu.CompilerParams(vmem_limit_bytes=56 * 1024 * 1024),
    )(*operands)


def norm_forward(rows, gain):
    scale = lax.rsqrt(jnp.mean(rows * rows, -1, keepdims=True) + EPS)
    return (rows * scale * gain).astype(jnp.bfloat16), scale


def norm_backward(rows, scale, gain, normed_grad):
    unit = rows * scale
    inward = normed_grad * gain
    rows_grad = scale * (inward - unit * jnp.mean(inward * unit, -1, keepdims=True))
    return rows_grad, jnp.sum(normed_grad * unit, (0, 1))


def gelu_parts(value):
    inner = math.sqrt(2 / math.pi) * (value + 0.044715 * value * value * value)
    curve = jnp.tanh(inner)
    activated = 0.5 * value * (1 + curve)
    slope = 0.5 * (1 + curve) + 0.5 * value * (1 - curve * curve) * math.sqrt(2 / math.pi) * (
        1 + 3 * 0.044715 * value * value
    )
    return activated, slope


def gather_rows(value):
    return lax.all_gather(value, "tensor", axis=1, tiled=True)


def scatter_rows(value):
    low = value.astype(jnp.bfloat16)
    return lax.psum_scatter(low, "tensor", scatter_dimension=1, tiled=True).astype(jnp.float32)


def gather_weight(pieces):
    return lax.all_gather(jnp.concatenate(pieces, 1), "dp", axis=0, tiled=True)


def scatter_weight(pieces):
    whole = jnp.concatenate(pieces, 1).astype(jnp.bfloat16)
    return lax.psum_scatter(whole, "dp", scatter_dimension=0, tiled=True).astype(jnp.float32)


def forward_product(rows, weight):
    return lax.dot_general(
        rows, weight, (((2,), (0,)), ((), ())), preferred_element_type=jnp.float32
    )


def back_product(rows, weight):
    return lax.dot_general(
        rows, weight, (((2,), (1,)), ((), ())), preferred_element_type=jnp.float32
    )


def weight_product(rows, gradient):
    return lax.dot_general(
        rows, gradient, (((0, 1), (0, 1)), ((), ())), preferred_element_type=jnp.float32
    )


def cut_columns(value, widths):
    parts, at = [], 0
    for width in widths:
        parts.append(value[..., at : at + width])
        at += width
    return parts


def on_device(
    states,
    encoder,
    upstream,
    decoder_docs,
    encoder_docs,
    norm_self,
    norm_cross,
    norm_feed,
    position_table,
    self_query,
    self_key,
    self_value,
    self_output,
    cross_query,
    cross_key,
    cross_value,
    cross_output,
    feed_gate,
    feed_up,
    feed_down,
):
    parts, _, width = states.shape
    length = decoder_docs.shape[1]
    encoder_length = encoder_docs.shape[1]
    inner = self_query.shape[1]
    hidden = feed_gate.shape[1]
    heads = inner // HEAD_DIM
    block = 256
    low = jnp.bfloat16

    self_in = gather_weight([self_query, self_key, self_value])
    middle = gather_weight([self_output.T, cross_query, cross_key, cross_value, cross_output.T])
    feed = gather_weight([feed_gate, feed_up, feed_down.T])
    self_out, query_cross, both_cross, cross_out = cut_columns(
        middle, (inner, inner, 2 * inner, inner)
    )
    feed_in, feed_out = cut_columns(feed, (2 * hidden, hidden))

    tensor_index = lax.axis_index("tensor")
    table = lax.dynamic_slice_in_dim(position_table, tensor_index * heads, heads, 1).T
    docs_column = decoder_docs[:, :, None]
    docs_row = decoder_docs[:, None, :]
    encoder_row = encoder_docs[:, None, :]

    residual = states.astype(jnp.float32)
    normed, scale_self = norm_forward(residual, norm_self)
    whole_self = gather_rows(normed)
    encoder_whole = gather_rows(encoder)
    upper = gather_rows(upstream)

    qkv = forward_product(whole_self, self_in).astype(low)
    log_shape = jax.ShapeDtypeStruct((parts, length, heads), jnp.float32)
    mixed_shape = jax.ShapeDtypeStruct((parts, length, inner), low)
    self_mixed, self_log = per_sequence(
        functools.partial(self_forward_kernel, heads, block),
        table,
        (docs_column, docs_row, qkv),
        (mixed_shape, log_shape),
    )
    residual_one = residual + scatter_rows(back_product(self_mixed, self_out))
    normed, scale_cross = norm_forward(residual_one, norm_cross)
    whole_cross = gather_rows(normed)
    both = forward_product(encoder_whole, both_cross).astype(low)
    queries = forward_product(whole_cross, query_cross).astype(low)
    cross_mixed, cross_log = per_sequence(
        functools.partial(cross_forward_kernel, heads, block),
        None,
        (docs_column, encoder_row, queries, both),
        (mixed_shape, log_shape),
    )
    residual_two = residual_one + scatter_rows(back_product(cross_mixed, cross_out))
    normed, scale_feed = norm_forward(residual_two, norm_feed)
    whole_feed = gather_rows(normed)
    gate, upward = cut_columns(forward_product(whole_feed, feed_in), (hidden, hidden))
    activated, slope = gelu_parts(gate)
    hidden_state = (activated * upward).astype(low)
    feed_result = scatter_rows(back_product(hidden_state, feed_out))
    layer_output = (residual_two + feed_result).astype(low)

    hidden_grad = forward_product(upper, feed_out)
    gate_grad = (hidden_grad * upward * slope).astype(low)
    up_grad = (hidden_grad * activated).astype(low)
    both_grad = jnp.concatenate([gate_grad, up_grad], 2)
    feed_grad = scatter_rows(back_product(both_grad, feed_in))
    feed_weights = scatter_weight(
        [weight_product(whole_feed, both_grad), weight_product(upper, hidden_state)]
    )
    step_grad, norm_feed_gradient = norm_backward(residual_two, scale_feed, norm_feed, feed_grad)
    grad_two = upstream.astype(jnp.float32) + step_grad

    upper_two = gather_rows(grad_two.astype(low))
    mixed_grad = forward_product(upper_two, cross_out).astype(low)
    query_grad, both_grad = per_sequence(
        functools.partial(cross_backward_kernel, heads, block),
        None,
        (docs_column, encoder_row, queries, both, cross_log, mixed_grad),
        (mixed_shape, jax.ShapeDtypeStruct((parts, encoder_length, 2 * inner), low)),
    )
    cross_grad = scatter_rows(back_product(query_grad, query_cross))
    encoder_gradient = scatter_rows(back_product(both_grad, both_cross))
    cross_query_whole = weight_product(whole_cross, query_grad)
    cross_both_whole = weight_product(encoder_whole, both_grad)
    cross_output_whole = weight_product(upper_two, cross_mixed)
    step_grad, norm_cross_gradient = norm_backward(residual_one, scale_cross, norm_cross, cross_grad)
    grad_one = grad_two + step_grad

    upper_one = gather_rows(grad_one.astype(low))
    self_output_whole = weight_product(upper_one, self_mixed)
    middle_weights = scatter_weight(
        [self_output_whole, cross_query_whole, cross_both_whole, cross_output_whole]
    )
    mixed_grad = forward_product(upper_one, self_out).astype(low)
    qkv_grad, diagonal = per_sequence(
        functools.partial(self_backward_kernel, heads, block),
        table,
        (docs_column, docs_row, qkv, self_log, mixed_grad),
        (
            jax.ShapeDtypeStruct((parts, length, 3 * inner), low),
            jax.ShapeDtypeStruct((parts, heads, 2 * block), jnp.float32),
        ),
    )
    normed_grad = scatter_rows(back_product(qkv_grad, self_in))
    self_weights = scatter_weight([weight_product(whole_self, qkv_grad)])
    step_grad, norm_self_gradient = norm_backward(residual, scale_self, norm_self, normed_grad)
    states_gradient = grad_one + step_grad

    count = distance_buckets(window_distance((1, 2 * block), 2 * block, block))
    onehot = (count == jnp.arange(BUCKETS, dtype=jnp.int32)[:, None]).astype(jnp.float32)
    table_local = jnp.dot(onehot, jnp.sum(diagonal, 0).T, precision=lax.Precision.HIGHEST)
    table_full = lax.dynamic_update_slice_in_dim(
        jnp.zeros(position_table.shape, jnp.float32), table_local, tensor_index * heads, 1
    )
    small = jnp.concatenate(
        [norm_self_gradient, norm_cross_gradient, norm_feed_gradient, table_full.reshape(-1)]
    )
    small = lax.psum(small, ("dp", "tensor"))

    query_self_g, key_self_g, value_self_g = cut_columns(self_weights, (inner,) * 3)
    self_out_g, query_cross_g, key_cross_g, value_cross_g, cross_out_g = cut_columns(
        middle_weights, (inner,) * 5
    )
    gate_g, up_g, down_g = cut_columns(feed_weights, (hidden,) * 3)
    return (
        layer_output,
        states_gradient,
        encoder_gradient,
        small[:width],
        small[width : 2 * width],
        small[2 * width : 3 * width],
        small[3 * width :].reshape(position_table.shape),
        query_self_g,
        key_self_g,
        value_self_g,
        self_out_g.T,
        query_cross_g,
        key_cross_g,
        value_cross_g,
        cross_out_g.T,
        gate_g,
        up_g,
        down_g.T,
    )


def solution(mesh):
    return jax.shard_map(
        on_device,
        mesh=mesh,
        in_specs=(
            P("dp", "tensor", None),
            P("dp", "tensor", None),
            P("dp", "tensor", None),
            P("dp", None),
            P("dp", None),
            P(),
            P(),
            P(),
            P(),
            P("dp", "tensor"),
            P("dp", "tensor"),
            P("dp", "tensor"),
            P("tensor", "dp"),
            P("dp", "tensor"),
            P("dp", "tensor"),
            P("dp", "tensor"),
            P("tensor", "dp"),
            P("dp", "tensor"),
            P("dp", "tensor"),
            P("tensor", "dp"),
        ),
        out_specs=(
            P("dp", "tensor", None),
            P("dp", "tensor", None),
            P("dp", "tensor", None),
            P(),
            P(),
            P(),
            P(),
            P("dp", "tensor"),
            P("dp", "tensor"),
            P("dp", "tensor"),
            P("tensor", "dp"),
            P("dp", "tensor"),
            P("dp", "tensor"),
            P("dp", "tensor"),
            P("tensor", "dp"),
            P("dp", "tensor"),
            P("dp", "tensor"),
            P("tensor", "dp"),
        ),
        check_vma=False,
    )
```

time: 1800 us -> 753 us (0.42)
  local copies, waits for them, and re-layouts: 351 us -> 23.2 us
  blocking collectives: 408 us -> 82.5 us
  waiting for transfers between devices: 781 us -> 498 us
  matrix products: 136 us -> 57.5 us
  loops' own time: 50.8 us -> 0 us
  Pallas kernels: 0 us -> 40.7 us
  other arithmetic: 48.5 us -> 26.2 us
    reduce_scatter x14 -> x9, waiting for transfers between devices: 617 us -> 289 us  [the longest x7 184 us: scatter_rows(): lax.psum_scatter(low, 'tensor', scatter_dimension=1, tiled=True)]
    all_gather x12 -> x2, blocking collectives: 367 us -> 43 us  [the longest x1 34.5 us: gather_weight(): return lax.all_gather(jnp.concatenate(pieces, 1), 'dp', axis=0, tiled=True)]
    while x78 -> x0, local copies, waits for them, and re-layouts: 170 us -> none
    reshape x6 -> x2, local copies, waits for them, and re-layouts: 89.1 us -> 0.2 us  [the longest x1 0.1 us: on_device(): table_full.reshape(-1)]
    dot_general x65 -> x22, matrix products: 130 us -> 57.5 us  [the longest x7 26.2 us: forward_product(): lax.dot_general(rows, weight, (((2,), (0,)), ((), ())), preferred_element...]
    all_gather x0 -> x2, waiting for transfers between devices: none -> 67.6 us  [gather_weight(): return lax.all_gather(jnp.concatenate(pieces, 1), 'dp', axis=0, tiled=True)]
    unnamed x28 -> x19, waiting for transfers between devices: 132 us -> 66.9 us
    another operation x4 -> x0, loops' own time: 50.8 us -> none  [the longest x2 40.8 us: attend_back(): lax.scan(one_block, (zeros, zeros, table_zero), blocks)]
  transfers between devices with their start and end apart: 24 -> 18, of which waited for: 17 -> 17; matrix products, arithmetic and copies ran while one was open for 18% -> 7% of each run, Pallas kernels for 0% -> 3%
where the time goes in v1:
time: 753 us; the launch traced here: 745 us
  waiting for transfers between devices  498 us (66%)
  blocking collectives  82.5 us (11%)
  matrix products  57.5 us (8%)
  Pallas kernels  40.7 us (5%)
  other arithmetic  26.2 us (3%)
  local copies, waits for them, and re-layouts  23.2 us (3%)
  between operations  15.3 us (2%)
    reduce_scatter x7, waiting for transfers between devices, scatter_rows(): lax.psum_scatter(low, 'tensor', scatter_dimension=1, tiled=True)  184 us
    reduce_scatter x2, waiting for transfers between devices, scatter_weight(): lax.psum_scatter(whole, 'dp', scatter_dimension=0, tiled=True)  105 us
    all_gather x6, waiting for transfers between devices, gather_rows(): return lax.all_gather(value, 'tensor', axis=1, tiled=True)  74.6 us
    all_gather x2, waiting for transfers between devices, gather_weight(): return lax.all_gather(jnp.concatenate(pieces, 1), 'dp', axis=0, tiled=True)  67.6 us
    unnamed x19, waiting for transfers between devices  66.9 us
    pallas_call x4, Pallas kernels, per_sequence(): pl.pallas_call(kernel, grid=(arrays[0].shape[0],), in_specs=ins, out_spec...  40.7 us
    psum x1, blocking collectives, on_device(): small = lax.psum(small, ('dp', 'tensor'))  39.5 us
    all_gather x1, blocking collectives, gather_weight(): return lax.all_gather(jnp.concatenate(pieces, 1), 'dp', axis=0, tiled=True)  34.5 us
  transfers between devices with their start and end apart: 18, of which 17 were waited for; matrix products, arithmetic and copies ran while one was open for 7% of the time, Pallas kernels for 3%

profile of v1, /device:TPU:0, one launch (start us, length us, event | category | flops | bytes accessed | tf_op | source)
XLA Modules:
  0.0 745.4 jit_solution(7394155119345193104)
XLA Ops:
  13.5 34.5 %all_gather.31 = bf16[768,576]{1,0:T(8,128)(2,1)S(1)} all-gather(bf16[96,576]{1,0:T(8,128)(2,1)S(1)} %pad_maximum_fusion.3), channel_id=1, replica_groups=mesh['dp'=8,'tensor'=4] {'dp'}, dimensions={0}, use_global_device_ids=true | all-gather | bytes 995328 | tf_op jit(solution)/shard_map/all_gather | solution.py:306
  52.2 9.9 %shard_map.331 = (bf16[1,1024,192]{2,1,0:T(8,128)(2,1)}, f32[1,1024,3]{2,1,0:T(8,128)}) custom-call(f32[3,32]{1,0:T(4,128)} %dynamic-slice_bitcast_fusion.table_ref, s32[1,1024,1]{2,1,0:T(8,128)} %copy.69.column_ref, s32[1,1,1024]{2,1,0:T(1,128)} %bitcast.160, bf16[1,1024,576]{2,1,0:T(8,128)(2,1)} %fusion.38.qkv_ref), custom_call_target="tpu_custom_call" | custom-call | tf_op jit(solution)/shard_map/pallas_call | solution.py:264
  62.1 17.9 %all-gather.11.cloned.1.call-done = bf16[768,960]{1,0:T(8,128)(2,1)} async-done(((bf16[96,960]{1,0:T(8,128)(2,1)}), bf16[768,960]{1,0:T(8,128)(2,1)}) %all-gather.11.cloned.1.call-update) | async-done | bytes 1474576 | tf_op jit(solution)/shard_map/all_gather | solution.py:306
  83.1 27.1 %reduce-scatter.13.cloned.1.call-done = bf16[1,256,768]{2,1,0:T(8,128)(2,1)} async-done(((bf16[1,1024,768]{2,1,0:T(8,128)(2,1)}), bf16[1,256,768]{2,1,0:T(8,128)(2,1)}) %reduce-scatter.13.cloned.1.call-update) | async-done | bytes 393232 | tf_op jit(solution)/shard_map/reduce_scatter | solution.py:302
  113.4 8.5 %all_gather.34 = bf16[1,512,768]{2,1,0:T(8,128)(2,1)S(1)} all-gather(bf16[1,128,768]{2,1,0:T(8,128)(2,1)S(1)} %copy-done.16), channel_id=1, replica_groups=mesh['dp'=8,'tensor'=4] {'tensor'}, dimensions={1}, use_global_device_ids=true | all-gather | bytes 983040 | tf_op jit(solution)/shard_map/all_gather | solution.py:297
  124.1 9.1 %all-gather.13.cloned.1.call-done = bf16[1,1024,768]{2,1,0:T(8,128)(2,1)} async-done(((bf16[1,256,768]{2,1,0:T(8,128)(2,1)}), bf16[1,1024,768]{2,1,0:T(8,128)(2,1)}) %all-gather.13.cloned.1.call-update) | async-done | bytes 1572880 | tf_op jit(solution)/shard_map/all_gather | solution.py:297
  136.1 8.2 %shard_map.332 = (bf16[1,1024,192]{2,1,0:T(8,128)(2,1)}, f32[1,1024,3]{2,1,0:T(8,128)}) custom-call(s32[1,1024,1]{2,1,0:T(8,128)} %copy.69.column_ref, s32[1,1,512]{2,1,0:T(1,128)} %bitcast.163, bf16[1,1024,192]{2,1,0:T(8,128)(2,1)} %fusion.68.query_ref, bf16[1,512,384]{2,1,0:T(8,128)(2,1)} %fusion.80.both_ref), custom_call_target="tpu_custom_call" | custom-call | tf_op jit(solution)/shard_map/pallas_call | solution.py:264
  148.0 27.4 %reduce-scatter.15.cloned.1.call-done = bf16[1,256,768]{2,1,0:T(8,128)(2,1)} async-done(((bf16[1,1024,768]{2,1,0:T(8,128)(2,1)}), bf16[1,256,768]{2,1,0:T(8,128)(2,1)}) %reduce-scatter.15.cloned.1.call-update) | async-done | bytes 393232 | tf_op jit(solution)/shard_map/reduce_scatter | solution.py:302
  179.9 49.7 %all-gather.17.cloned.1.call-done = bf16[768,1536]{1,0:T(8,128)(2,1)} async-done(((bf16[96,1536]{1,0:T(8,128)(2,1)}), bf16[768,1536]{1,0:T(8,128)(2,1)}) %all-gather.17.cloned.1.call-update) | async-done | bytes 2359312 | tf_op jit(solution)/shard_map/all_gather | solution.py:306
  229.6 20.4 %all-gather.15.cloned.1.call-done = bf16[1,1024,768]{2,1,0:T(8,128)(2,1)} async-done(((bf16[1,256,768]{2,1,0:T(8,128)(2,1)}), bf16[1,1024,768]{2,1,0:T(8,128)(2,1)}) %all-gather.15.cloned.1.call-update) | async-done | bytes 1572880 | tf_op jit(solution)/shard_map/all_gather | solution.py:297
  255.7 15.5 %all-gather.19.cloned.1.call-done = bf16[1,1024,768]{2,1,0:T(8,128)(2,1)} async-done(((bf16[1,256,768]{2,1,0:T(8,128)(2,1)}), bf16[1,1024,768]{2,1,0:T(8,128)(2,1)}) %all-gather.19.cloned.1.call-update) | async-done | bytes 1572880 | tf_op jit(solution)/shard_map/all_gather | solution.py:297
  282.1 28.3 %reduce-scatter.19.cloned.1.call-done = bf16[1,256,768]{2,1,0:T(8,128)(2,1)} async-done(((bf16[1,1024,768]{2,1,0:T(8,128)(2,1)}), bf16[1,256,768]{2,1,0:T(8,128)(2,1)}) %reduce-scatter.19.cloned.1.call-update) | async-done | bytes 393232 | tf_op jit(solution)/shard_map/reduce_scatter | solution.py:302
  315.1 19.6 %all-gather.21.cloned.1.call-done = bf16[1,1024,768]{2,1,0:T(8,128)(2,1)} async-done(((bf16[1,256,768]{2,1,0:T(8,128)(2,1)}), bf16[1,1024,768]{2,1,0:T(8,128)(2,1)}) %all-gather.21.cloned.1.call-update) | async-done | bytes 1572880 | tf_op jit(solution)/shard_map/all_gather | solution.py:297
  337.5 9.7 %shard_map.333 = (bf16[1,1024,192]{2,1,0:T(8,128)(2,1)}, bf16[1,512,384]{2,1,0:T(8,128)(2,1)}) custom-call(s32[1,1024,1]{2,1,0:T(8,128)} %copy.69.column_ref, s32[1,1,512]{2,1,0:T(1,128)} %bitcast.164, bf16[1,1024,192]{2,1,0:T(8,128)(2,1)} %fusion.68.query_ref, bf16[1,512,384]{2,1,0:T(8,128)(2,1)} %fusion.80.both_ref, ...), custom_call_target="tpu_custom_call" | custom-call | tf_op jit(solution)/shard_map/pallas_call | solution.py:264
  354.8 23.7 %reduce-scatter.21.cloned.1.call-done = bf16[1,256,768]{2,1,0:T(8,128)(2,1)} async-done(((bf16[1,1024,768]{2,1,0:T(8,128)(2,1)}), bf16[1,256,768]{2,1,0:T(8,128)(2,1)}) %reduce-scatter.21.cloned.1.call-update) | async-done | bytes 393232 | tf_op jit(solution)/shard_map/reduce_scatter | solution.py:302
  380.0 29.2 %reduce-scatter.17.cloned.1.call-done = bf16[1,256,768]{2,1,0:T(8,128)(2,1)} async-done(((bf16[1,1024,768]{2,1,0:T(8,128)(2,1)}), bf16[1,256,768]{2,1,0:T(8,128)(2,1)}) %reduce-scatter.17.cloned.1.call-update) | async-done | bytes 393232 | tf_op jit(solution)/shard_map/reduce_scatter | solution.py:302
  421.6 10.1 %all-gather.23.cloned.1.call-done = bf16[1,1024,768]{2,1,0:T(8,128)(2,1)} async-done(((bf16[1,256,768]{2,1,0:T(8,128)(2,1)}), bf16[1,1024,768]{2,1,0:T(8,128)(2,1)}) %all-gather.23.cloned.1.call-update) | async-done | bytes 1572880 | tf_op jit(solution)/shard_map/all_gather | solution.py:297
  434.4 12.9 %shard_map.334 = (bf16[1,1024,576]{2,1,0:T(8,128)(2,1)}, f32[1,3,512]{2,1,0:T(4,128)}) custom-call(f32[3,32]{1,0:T(4,128)} %dynamic-slice_bitcast_fusion.table_ref, s32[1,1024,1]{2,1,0:T(8,128)} %copy.69.column_ref, s32[1,1,1024]{2,1,0:T(1,128)} %bitcast.161, bf16[1,1024,576]{2,1,0:T(8,128)(2,1)} %fusion.38.qkv_ref, ...), custom_call_target="tpu_custom_call" | custom-call | tf_op jit(solution)/shard_map/pallas_call | solution.py:264
  463.7 40.7 %reduce-scatter.29.cloned.1.call-done = bf16[96,1536]{1,0:T(8,128)(2,1)} async-done(((bf16[768,1536]{1,0:T(8,128)(2,1)}), bf16[96,1536]{1,0:T(8,128)(2,1)}) %reduce-scatter.29.cloned.1.call-update) | async-done | bytes 294928 | tf_op jit(solution)/shard_map/reduce_scatter | solution.py:311
  507.2 22.7 %reduce-scatter.25.cloned.1.call-done = bf16[1,128,768]{2,1,0:T(8,128)(2,1)} async-done(((bf16[1,512,768]{2,1,0:T(8,128)(2,1)}), bf16[1,128,768]{2,1,0:T(8,128)(2,1)}) %reduce-scatter.25.cloned.1.call-update) | async-done | bytes 196624 | tf_op jit(solution)/shard_map/reduce_scatter | solution.py:302
  532.2 64.4 %reduce-scatter.27.cloned.1.call-done = bf16[96,576]{1,0:T(8,128)(2,1)} async-done(((bf16[768,576]{1,0:T(8,128)(2,1)}), bf16[96,576]{1,0:T(8,128)(2,1)}) %reduce-scatter.27.cloned.1.call-update) | async-done | bytes 110608 | tf_op jit(solution)/shard_map/reduce_scatter | solution.py:311
  598.2 65.9 %reduce-scatter.31.cloned.1.call-done = bf16[96,960]{1,0:T(8,128)(2,1)} async-done(((bf16[768,960]{1,0:T(8,128)(2,1)}), bf16[96,960]{1,0:T(8,128)(2,1)}) %reduce-scatter.31.cloned.1.call-update) | async-done | bytes 184336
  668.2 25.5 %reduce-scatter.23.cloned.1.call-done = bf16[1,256,768]{2,1,0:T(8,128)(2,1)} async-done(((bf16[1,1024,768]{2,1,0:T(8,128)(2,1)}), bf16[1,256,768]{2,1,0:T(8,128)(2,1)}) %reduce-scatter.23.cloned.1.call-update) | async-done | bytes 393232 | tf_op jit(solution)/shard_map/reduce_scatter | solution.py:302
  695.1 39.5 %psum.7 = f32[2688]{0:T(1024)S(1)} all-reduce(f32[2688]{0:T(1024)S(1)} %pad_maximum_fusion.4), channel_id=1, replica_groups=mesh['dp'=8,'tensor'=4] {'dp','tensor'}, use_global_device_ids=true, to_apply=%region_16.0 | all-reduce | flops 2688 | bytes 21504 | tf_op jit(solution)/shard_map/psum | solution.py:476
  (213 shorter events, 109.8 us)
Async XLA Ops:
  7.3 40.7 %all-gather.9.cloned.1.call-start = ((), (), s32[]{:S(2)}) async-start(), calls=%async_computation.10 | async-start | bytes 1966080 | tf_op jit(solution)/shard_map/all_gather | solution.py:297
  10.5 69.5 %all-gather.11.cloned.1.call-start = ((), (), s32[]{:S(2)}) async-start(), calls=%async_computation.11 | async-start | bytes 1769472 | tf_op jit(solution)/shard_map/all_gather | solution.py:306
  11.7 98.5 %reduce-scatter.13.cloned.1.call-start = ((), (), s32[]{:S(2)}) async-start(), calls=%async_computation.12 | async-start | bytes 1966080 | tf_op jit(solution)/shard_map/reduce_scatter | solution.py:302
  83.0 50.1 %all-gather.13.cloned.1.call-start = ((), (), s32[]{:S(2)}) async-start(), calls=%async_computation.13 | async-start | bytes 1966080 | tf_op jit(solution)/shard_map/all_gather | solution.py:297
  113.4 62.1 %reduce-scatter.15.cloned.1.call-start = ((), (), s32[]{:S(2)}) async-start(), calls=%async_computation.14 | async-start | bytes 1966080 | tf_op jit(solution)/shard_map/reduce_scatter | solution.py:302
  147.1 82.5 %all-gather.17.cloned.1.call-start = ((), (), s32[]{:S(2)}) async-start(), calls=%async_computation.16 | async-start | bytes 2654208 | tf_op jit(solution)/shard_map/all_gather | solution.py:306
  148.0 102.0 %all-gather.15.cloned.1.call-start = ((), (), s32[]{:S(2)}) async-start(), calls=%async_computation.15 | async-start | bytes 1966080 | tf_op jit(solution)/shard_map/all_gather | solution.py:297
  176.7 79.0 %copy-start.32 = (f32[256]{0:T(256)}, f32[256]{0:T(256)S(1)}, u32[]{:S(2)}) copy-start(f32[256]{0:T(256)S(1)} %add_rsqrt_fusion) | copy-start | bytes 3076
  178.7 92.5 %all-gather.19.cloned.1.call-start = ((), (), s32[]{:S(2)}) async-start(), calls=%async_computation.18 | async-start | bytes 1966080 | tf_op jit(solution)/shard_map/all_gather | solution.py:297
  179.5 130.9 %reduce-scatter.19.cloned.1.call-start = ((), (), s32[]{:S(2)}) async-start(), calls=%async_computation.19 | async-start | bytes 1966080 | tf_op jit(solution)/shard_map/reduce_scatter | solution.py:302
  282.1 52.6 %all-gather.21.cloned.1.call-start = ((), (), s32[]{:S(2)}) async-start(), calls=%async_computation.20 | async-start | bytes 1966080 | tf_op jit(solution)/shard_map/all_gather | solution.py:297
  314.9 63.7 %reduce-scatter.21.cloned.1.call-start = ((), (), s32[]{:S(2)}) async-start(), calls=%async_computation.21 | async-start | bytes 1966080 | tf_op jit(solution)/shard_map/reduce_scatter | solution.py:302
  350.2 58.9 %reduce-scatter.17.cloned.1.call-start = ((), (), s32[]{:S(2)}) async-start(), calls=%async_computation.17 | async-start | bytes 1966080 | tf_op jit(solution)/shard_map/reduce_scatter | solution.py:302
  354.7 54.4 %copy-start.33 = (f32[256]{0:T(256)S(1)}, f32[256]{0:T(256)}, u32[]{:S(2)}) copy-start(f32[256]{0:T(256)} %copy-done.32) | copy-start | bytes 3076
  354.7 54.4 %copy-start.40 = (f32[256]{0:T(256)S(1)}, f32[256]{0:T(256)}, u32[]{:S(2)}) copy-start(f32[256]{0:T(256)} %copy-done.39) | copy-start | bytes 3076
  354.8 76.9 %all-gather.23.cloned.1.call-start = ((), (), s32[]{:S(2)}) async-start(), calls=%async_computation.22 | async-start | bytes 1966080 | tf_op jit(solution)/shard_map/all_gather | solution.py:297
  411.8 92.6 %reduce-scatter.29.cloned.1.call-start = ((), (), s32[]{:S(2)}) async-start(), calls=%async_computation.26 | async-start | bytes 2654208 | tf_op jit(solution)/shard_map/reduce_scatter | solution.py:311
  418.3 111.6 %reduce-scatter.25.cloned.1.call-start = ((), (), s32[]{:S(2)}) async-start(), calls=%async_computation.24 | async-start | bytes 983040 | tf_op jit(solution)/shard_map/reduce_scatter | solution.py:302
  421.3 175.2 %reduce-scatter.27.cloned.1.call-start = ((), (), s32[]{:S(2)}) async-start(), calls=%async_computation.25 | async-start | bytes 1105920 | tf_op jit(solution)/shard_map/reduce_scatter | solution.py:311
  451.2 212.9 %reduce-scatter.31.cloned.1.call-start = ((), (), s32[]{:S(2)}) async-start(), calls=%async_computation.27 | async-start | bytes 1769472
  458.5 235.2 %reduce-scatter.23.cloned.1.call-start = ((), (), s32[]{:S(2)}) async-start(), calls=%async_computation.23 | async-start | bytes 1966080 | tf_op jit(solution)/shard_map/reduce_scatter | solution.py:302
  463.6 68.0 %copy-start.47 = (f32[1,3,512]{2,1,0:T(4,128)S(1)}, f32[1,3,512]{2,1,0:T(4,128)}, u32[]{:S(2)}) copy-start(f32[1,3,512]{2,1,0:T(4,128)} %get-tuple-element.33) | copy-start | bytes 18436
  532.2 161.5 %copy-start.31 = (f32[768]{0:T(1024)S(1)}, f32[768]{0:T(1024)}, u32[]{:S(2)}) copy-start(f32[768]{0:T(1024)} %param.25) | copy-start | bytes 9220
  532.2 161.5 %copy-start.35 = (f32[256]{0:T(256)S(1)}, f32[256]{0:T(256)}, u32[]{:S(2)}) copy-start(f32[256]{0:T(256)} %copy-done.34) | copy-start | bytes 3076
  (47 other events, 426.8 us)
Sparse Core Ops, SparseCore 0:
  10.6 22.3 all-gather.8
  35.8 44.1 all-gather.10
  83.1 26.9 reduce-scatter.12
  113.5 19.6 all-gather.12
  147.3 28.1 reduce-scatter.14
  177.5 52.0 all-gather.16
  231.8 18.1 all-gather.14
  251.5 19.6 all-gather.18
  282.2 28.1 reduce-scatter.18
  315.0 19.6 all-gather.20
  350.3 28.1 reduce-scatter.20
  380.9 28.1 reduce-scatter.16
  411.9 19.6 all-gather.22
  435.4 68.9 reduce-scatter.28
  507.5 22.3 reduce-scatter.24
  533.1 63.3 reduce-scatter.26
  600.2 63.8 reduce-scatter.30
  666.5 27.1 reduce-scatter.22
